TPU v7x, 32 devices: a whole 2x2x4 slice. The times are simulated.
32 devices in a mesh: parts: 2 (over x), tp: 16 (over z, y, core).
Axes of the slice: x: 2, y: 2, z: 4, core: 2. Of those that a mesh axis runs over, the one named last changes fastest.
Arguments:
- x_in: bfloat16 [64, 4, 5120], P('parts', None, 'tp'), parts along dimension 0, may hold values from -6 to 6
- ln_gain: bfloat16 [5120], P('tp'), may hold values from 0.5 to 1.5
- w_query: bfloat16 [5120, 8192], P(None, 'tp'), may hold values from -0.078125 to 0.078125
- w_key: bfloat16 [5120, 1024], P(None, 'tp'), may hold values from -0.078125 to 0.078125
- w_value: bfloat16 [5120, 1024], P(None, 'tp'), may hold values from -0.078125 to 0.078125
- w_out: bfloat16 [8192, 5120], P('tp'), may hold values from -0.0625 to 0.0625
- q_gain: bfloat16 [128], replicated, may hold values from 0.5 to 1.5
- k_gain: bfloat16 [128], replicated, may hold values from 0.5 to 1.5
- a_query: bfloat16 [5120, 64], P('tp'), may hold values from -0.078125 to 0.078125
- a_key: bfloat16 [5120, 64], P('tp'), may hold values from -0.078125 to 0.078125
- a_value: bfloat16 [5120, 64], P('tp'), may hold values from -0.078125 to 0.078125
- b_query: bfloat16 [64, 8192], P(None, 'tp'), may hold values from -0.75 to 0.75
- b_key: bfloat16 [64, 1024], P(None, 'tp'), may hold values from -0.75 to 0.75
- b_value: bfloat16 [64, 1024], P(None, 'tp'), may hold values from -0.75 to 0.75
- a_out: bfloat16 [8192, 64], P('tp'), may hold values from -0.0625 to 0.0625
- b_out: bfloat16 [64, 5120], P(None, 'tp'), may hold values from -0.75 to 0.75
- key_cache: bfloat16 [64, 1024, 1024], P(('parts', 'tp')), parts along dimension 0, may hold values from -2.5 to 2.5
- value_cache: bfloat16 [64, 1024, 1024], P(('parts', 'tp')), parts along dimension 0, may hold values from -2.5 to 2.5
- kv_length: int32 [64], P(('parts', 'tp')), parts along dimension 0, may hold values from 1 to 1024, as said below
- cand_rows: bfloat16 [64, 8, 5120], P(('parts', 'tp')), parts along dimension 0, may hold values from -0.078125 to 0.078125
- final_gain: bfloat16 [5120], replicated, may hold values from 0.099609375 to 1.8984375
- row_owner: int32 [64, 1], P('parts'), parts along dimension 0, may hold values from 0 to 15; in each aligned block of 32 rows (0 to 31, 32 to 63, ...) at most 4 rows name the same one
Outputs:
- hidden_out: bfloat16 [64, 4, 5120], P(('parts', 'tp')), parts along dimension 0
- cand_logprob: float32 [128, 32], P(('parts', 'tp')), parts along dimension 0
There are 2 independent parts, one for each index of `parts`. A program takes and returns all parts, laid end to end along the dimension named above; an argument that names none is the same for every part. Nothing has to cross between parts.
Inputs may be any that keep to these rules, and one draw needn't show every extreme that they name: `kv_length`: one row holds exactly 1024 cached positions and another exactly 1. `row_owner`: no tp index owns more than 4 rows, some owns exactly 4, and every index owns at least one.
All inputs are finite; a program needn't handle non-finite values.
Results may differ from a plain program's by a relative error of at most 0.007.
Values may be sent and summed in bfloat16 or wider, within the bound.
A program may use at most 128 MiB of HBM per device.

v0:
```python
import math

import jax
import jax.numpy as jnp
from jax import lax
from jax.sharding import PartitionSpec as P

CAP = 4


EPSILON = 1e-06
ROPE_BASE = 1000000.0


def scale_of(values):
    return lax.rsqrt(jnp.mean(values * values, axis=-1, keepdims=True) + EPSILON)


def rotary(values, position):
    half_size = values.shape[-1] // 2
    frequency = ROPE_BASE ** (-jnp.arange(half_size, dtype=jnp.float32) / half_size)
    angles = position.astype(jnp.float32)[:, :, None, None] * frequency
    angles = jnp.concatenate([angles, angles], axis=-1)
    turned = jnp.concatenate([-values[..., half_size:], values[..., :half_size]], axis=-1)
    return values * jnp.cos(angles) + turned * jnp.sin(angles)


def head_norm(values, gain_vec, position):
    floated = values.astype(jnp.float32)
    return rotary(floated * scale_of(floated) * gain_vec.astype(jnp.float32), position).astype(
        jnp.bfloat16
    )


def live_mask(lengths, span_len, step_count):
    column = jnp.arange(span_len + step_count, dtype=jnp.int32)[None, None, :]
    step_ids = jnp.arange(step_count, dtype=jnp.int32)[None, :, None]
    cached = (column < lengths[:, None, None]) & (column < span_len)
    fresh = (column >= span_len) & (column - span_len <= step_ids)
    return (cached | fresh).astype(jnp.float32)


def slot_of(row_owner, shards, capacity):
    owned_rows = (row_owner[:, None] == jnp.arange(shards, dtype=jnp.int32)[None, :]).astype(
        jnp.int32
    )
    before = jnp.cumsum(owned_rows, axis=0) - owned_rows
    return row_owner * capacity + jnp.sum(before * owned_rows, axis=1)


def exact_dot(left, right):
    return jnp.dot(left, right.astype(jnp.float32), precision=lax.Precision.HIGHEST)


def attend(queries, new_keys, new_values, key_cache, value_cache, lengths):
    row_count, step_count, head_count, head_size = queries.shape
    group_count = new_keys.shape[2]
    span_len = key_cache.shape[1]
    key_all = jnp.concatenate(
        [key_cache, new_keys.reshape(row_count, step_count, group_count * head_size)], axis=1
    )
    value_all = jnp.concatenate([value_cache, new_values], axis=1)
    key_all = key_all.reshape(row_count, span_len + step_count, group_count, head_size)
    value_all = value_all.reshape(row_count, span_len + step_count, group_count, head_size)
    grouped = queries.reshape(
        row_count, step_count, group_count, head_count // group_count, head_size
    )
    scores = jnp.einsum(
        "rsngd,rtnd->rsngt", grouped, key_all, preferred_element_type=jnp.float32
    ) / math.sqrt(head_size)
    weights = jnp.exp(scores) * live_mask(lengths, span_len, step_count)[:, :, None, None, :]
    weights = (weights / jnp.sum(weights, axis=-1, keepdims=True)).astype(jnp.bfloat16)
    mixed_heads = jnp.einsum(
        "rsngt,rtnd->rsngd", weights, value_all, preferred_element_type=jnp.float32
    )
    return mixed_heads.reshape(row_count, step_count, head_count * head_size).astype(jnp.bfloat16)


def on_device(
    x_in,
    ln_gain,
    w_query,
    w_key,
    w_value,
    w_out,
    q_gain,
    k_gain,
    a_query,
    a_key,
    a_value,
    b_query,
    b_key,
    b_value,
    a_out,
    b_out,
    key_cache,
    value_cache,
    kv_length,
    cand_rows,
    final_gain,
    row_owner,
):
    shards = lax.axis_size("tp")
    device_index = lax.axis_index("tp")
    row_count, step_count, part_width = x_in.shape
    full_width = part_width * shards
    local_rows = row_count // shards
    head_size = q_gain.shape[0]
    head_cols = w_query.shape[1]
    kv_cols = w_key.shape[1]
    rank_size = a_query.shape[1]
    x_float = x_in.astype(jnp.float32)
    squares = lax.psum(jnp.sum(x_float * x_float, axis=-1), "tp")
    inverse = lax.rsqrt(squares / full_width + EPSILON)[..., None]
    normed = (x_float * inverse * ln_gain.astype(jnp.float32)).astype(jnp.bfloat16)
    flat_normed = normed.reshape(row_count * step_count, part_width)
    base_weight = jnp.concatenate([w_query, w_key, w_value], axis=1)
    partial_low = jnp.concatenate(
        [
            jnp.dot(flat_normed, a_query, preferred_element_type=jnp.float32),
            jnp.dot(flat_normed, a_key, preferred_element_type=jnp.float32),
            jnp.dot(flat_normed, a_value, preferred_element_type=jnp.float32),
        ],
        axis=1,
    )
    low_full = lax.psum(partial_low, "tp")
    weight_parts = (base_weight,)
    lifted = jnp.concatenate(
        [
            exact_dot(low_full[:, :rank_size], b_query),
            exact_dot(low_full[:, rank_size : 2 * rank_size], b_key),
            exact_dot(low_full[:, 2 * rank_size :], b_value),
        ],
        axis=1,
    )
    part_weight = weight_parts[0]
    running = jnp.dot(
        lax.all_gather(flat_normed, "tp", axis=1, tiled=True),
        part_weight,
        preferred_element_type=jnp.float32,
    )
    projected = running + lifted
    mixed_proj = projected.astype(jnp.bfloat16).reshape(
        row_count, step_count, head_cols + 2 * kv_cols
    )
    by_row = lax.all_to_all(mixed_proj, "tp", split_axis=0, concat_axis=2, tiled=True)
    by_row = by_row.reshape(local_rows, step_count, shards, head_cols + 2 * kv_cols)
    query_lin = by_row[..., :head_cols].reshape(local_rows, step_count, -1, head_size)
    key_lin = by_row[..., head_cols : head_cols + kv_cols].reshape(
        local_rows, step_count, -1, head_size
    )
    value_lin = by_row[..., head_cols + kv_cols :].reshape(local_rows, step_count, shards * kv_cols)
    position = kv_length[:, None] + jnp.arange(step_count, dtype=jnp.int32)[None, :]
    queries = head_norm(query_lin, q_gain, position)
    new_keys = head_norm(key_lin, k_gain, position)
    attended = attend(queries, new_keys, value_lin, key_cache, value_cache, kv_length)
    by_head = lax.all_to_all(attended, "tp", split_axis=2, concat_axis=0, tiled=True)
    up_full = lax.all_gather(b_out, "tp", axis=1, tiled=True)
    segment = by_head.reshape(lax.axis_size("tp") * local_rows * step_count, head_cols)
    summed = lax.psum_scatter(
        (
            jnp.dot(segment, w_out, preferred_element_type=jnp.float32)
            + exact_dot(jnp.dot(segment, a_out, preferred_element_type=jnp.float32), up_full)
        ).reshape(lax.axis_size("tp") * local_rows, step_count, full_width),
        "tp",
        scatter_dimension=0,
        tiled=True,
    )
    residual = lax.all_to_all(x_in, "tp", split_axis=0, concat_axis=2, tiled=True)
    hidden_out = (residual.astype(jnp.float32) + summed).astype(jnp.bfloat16)
    hidden_float = hidden_out.astype(jnp.float32)
    final_normed = (hidden_float * scale_of(hidden_float) * final_gain.astype(jnp.float32)).astype(
        jnp.bfloat16
    )
    logits = jnp.einsum("rsd,rkd->rsk", final_normed, cand_rows, preferred_element_type=jnp.float32)
    logprob = logits - jnp.log(jnp.sum(jnp.exp(logits), axis=-1, keepdims=True))
    logprob = logprob.reshape(local_rows, step_count * cand_rows.shape[1])
    slot_index = slot_of(row_owner[:, 0], shards, CAP)
    all_rows = lax.all_gather(logprob, "tp", axis=0, tiled=True)
    wanted = device_index * CAP + jnp.arange(CAP, dtype=jnp.int32)
    select = (slot_index[None, :] == wanted[:, None]).astype(jnp.float32)
    cand_logprob = jnp.dot(select, all_rows, precision=lax.Precision.HIGHEST)
    return (hidden_out, cand_logprob)


def solution(mesh):
    placed = (
        P("parts", None, "tp"),
        P("tp"),
        P(None, "tp"),
        P(None, "tp"),
        P(None, "tp"),
        P("tp", None),
        P(),
        P(),
        P("tp", None),
        P("tp", None),
        P("tp", None),
        P(None, "tp"),
        P(None, "tp"),
        P(None, "tp"),
        P("tp", None),
        P(None, "tp"),
        P(("parts", "tp"), None, None),
        P(("parts", "tp"), None, None),
        P(("parts", "tp")),
        P(("parts", "tp"), None, None),
        P(),
        P("parts", None),
    )
    return jax.shard_map(
        on_device,
        mesh=mesh,
        in_specs=placed,
        out_specs=(P(("parts", "tp"), None, None), P(("parts", "tp"), None)),
        check_vma=False,
    )
```

profile of v0, /device:TPU:0, one launch (start us, length us, event | category | flops | bytes accessed | tf_op | source)
XLA Modules:
  0.0 399.3 jit_solution(14482179803442704647)
XLA Ops:
  8.4 34.9 %psum.14 = f32[32,4]{0,1:T(4,128)S(1)} all-reduce(f32[32,4]{0,1:T(4,128)S(1)} %copy.108), channel_id=1, replica_groups=mesh['parts'=2,'tp'=16] {'tp'}, use_global_device_ids=true, to_apply=%region_1.0 | all-reduce | flops 128 | bytes 1024 | tf_op jit(solution)/shard_map/psum | solution.py:113
  52.9 6.2 %copy.118 = bf16[2,1024,1024]{1,2,0:T(8,128)(2,1)} copy(bf16[2,1024,1024]{2,1,0:T(8,128)(2,1)} %param.38) | data formatting | bytes 8388608 | tf_op args[16]
  59.1 6.2 %copy.122 = bf16[2,1024,8,128]{3,1,2,0:T(8,128)(2,1)} copy(bf16[2,1024,8,128]{1,3,2,0:T(8,128)(2,1)} %bitcast.92) | data formatting | bytes 8388608 | tf_op jit(solution)/shard_map/concatenate | solution.py:59
  65.3 6.3 %copy.107 = bf16[2,1024,1024]{1,2,0:T(8,128)(2,1)} copy(bf16[2,1024,1024]{2,1,0:T(8,128)(2,1)} %param.39) | data formatting | bytes 8388608 | tf_op args[17]
  71.6 6.3 %copy.116 = bf16[2,1024,8,128]{3,1,2,0:T(8,128)(2,1)} copy(bf16[2,1024,8,128]{1,3,2,0:T(8,128)(2,1)} %bitcast.93) | data formatting | bytes 8388608 | tf_op jit(solution)/shard_map/concatenate | solution.py:62
  78.3 55.0 %all-reduce.4.cloned.1.call-done = f32[128,192]{0,1:T(8,128)} async-done(((f32[128,192]{0,1:T(8,128)}), f32[128,192]{0,1:T(8,128)}) %all-reduce.4.cloned.1.call-update) | async-done | bytes 98320 | tf_op jit(solution)/shard_map/psum | solution.py:126
  136.3 37.8 %all-gather.4.cloned.1.call-done = bf16[128,5120]{0,1:T(8,128)(2,1)} async-done(((bf16[128,320]{0,1:T(8,128)(2,1)}), bf16[128,5120]{0,1:T(8,128)(2,1)}) %all-gather.4.cloned.1.call-update) | async-done | bytes 1310736 | tf_op jit(solution)/shard_map/all_gather | solution.py:138
  174.2 4.3 %fusion.22 = bf16[128,640]{1,0:T(8,128)(2,1)S(1)} fusion(bf16[128,5120]{0,1:T(8,128)(2,1)} %all-gather.4.cloned.1.call-done, bf16[5120,64]{1,0:T(8,128)(2,1)S(1)} %copy.112, bf16[5120,64]{1,0:T(8,128)(2,1)S(1)} %copy.111, bf16[5120,512]{1,0:T(8,128)(2,1)} %param.24, f32[128,64]{1,0:T(8,128)S(1)} %fusion.44, f32[128,64]{1,0:T(8,128)S(1)} %fusion.46, ...), kind=kOutput, calls=%fused_computation.23 | convolution fusion | flops 858849280 | bytes 8355840 | tf_op jit(solution)/shard_map/dot_general | solution.py:137
  179.2 3.5 all-to-all-start.1
  182.7 8.4 %all-to-all-done.1 = bf16[32,4,640]{2,1,0:T(4,128)(2,1)S(1)} async-done(((bf16[32,4,640]{2,1,0:T(4,128)(2,1)}), bf16[32,4,640]{2,1,0:T(4,128)(2,1)S(1)}, u32[]{:S(2)}, u32[]{:S(2)}) %all-to-all-start.1) | async-done | bytes 163872 | tf_op jit(solution)/shard_map/all_to_all | solution.py:146
  192.6 5.2 %fusion.16 = f32[2,4,8,8,1028]{4,3,1,2,0:T(8,128)} fusion(bf16[2,4,8,128]{3,1,2,0:T(4,128)(2,1)S(1)} %fusion.51, bf16[2,1024,8,128]{3,1,2,0:T(8,128)(2,1)} %copy.122, f32[2,4,1028]{2,1,0:T(4,128)S(1)} %or_convert_fusion, f32[2,4,8,8,64]{4,3,2,1,0:T(8,128)S(1)} %get-tuple-element.5, f32[2,4,8,8,64]{4,3,2,1,0:T(8,128)S(1)} %get-tuple-element.4, ...), kind=kOutput, calls=%fused_computation.19 | convolution fusion | flops 144674816 | bytes 6883968 | tf_op jit(solution)/shard_map/rsngd,rtnd->rsngt/dot_general | solution.py:68
  197.8 4.5 %fusion.26 = bf16[2,4,8,8,128]{4,3,1,2,0:T(8,128)(2,1)S(1)} fusion(f32[2,4,8,8,1028]{4,3,1,2,0:T(8,128)} %fusion.16, bf16[2,4,8,128]{3,1,2,0:T(4,128)(2,1)S(1)} %copy.117, bf16[2,1024,8,128]{3,1,2,0:T(8,128)(2,1)} %copy.116), kind=kOutput, calls=%fused_computation.25 | convolution fusion | flops 144283136 | bytes 6447104 | tf_op jit(solution)/shard_map/rsngt,rtnd->rsngd/dot_general | solution.py:73
  202.4 4.9 %copy.133 = bf16[2,4,8,8,128]{1,0,4,3,2:T(2,128)(2,1)} copy(bf16[2,4,8,8,128]{4,3,1,2,0:T(8,128)(2,1)S(1)} %fusion.26) | data formatting | bytes 262144 | tf_op jit(solution)/shard_map/convert_element_type | solution.py:76
  207.3 9.3 %reshape.288 = bf16[16,2,2048]{2,1,0:T(2,128)(2,1)} reshape(bf16[8192,2,4]{2,1,0:T(2,128)(2,1)} %bitcast.90) | data formatting | bytes 262144
  216.6 3.5 all-to-all-start.2
  220.1 24.1 %all-gather = bf16[16,320,64]{1,2,0:T(8,128)(2,1)S(1)} all-gather(bf16[1,320,64]{1,2,0:T(8,128)(2,1)S(1)} %bitcast.101), channel_id=1, replica_groups=mesh['parts'=2,'tp'=16] {'tp'}, dimensions={0}, use_global_device_ids=true | all-gather | bytes 696320 | tf_op jit(solution)/shard_map/all_gather | solution.py:158
  245.3 10.0 %reshape.289 = bf16[8192,2,4]{2,1,0:T(2,128)(2,1)} reshape(bf16[16,2,2048]{2,1,0:T(2,128)(2,1)S(1)} %all-to-all-done.2) | data formatting | bytes 262144
  255.3 9.7 %copy.126 = bf16[2,4,16,512]{3,1,0,2:T(4,128)(2,1)S(1)} copy(bf16[2,4,16,512]{1,0,3,2:T(2,128)(2,1)} %bitcast.91) | data formatting | bytes 262144 | tf_op jit(solution)/shard_map/all_to_all | solution.py:157
  265.1 3.4 fusion.73
  270.0 1.9 reshape.273
  272.0 3.5 all-to-all-start
  277.1 7.6 %all-to-all-done = bf16[32,4,320]{2,1,0:T(4,128)(2,1)S(1)} async-done(((bf16[32,4,320]{2,1,0:T(4,128)(2,1)}), bf16[32,4,320]{2,1,0:T(4,128)(2,1)S(1)}, u32[]{:S(2)}, u32[]{:S(2)}) %all-to-all-start) | async-done | bytes 81952 | tf_op jit(solution)/shard_map/all_to_all | solution.py:169
  284.9 85.9 %all-reduce.6.cloned.1.call-done = f32[32,4,5120]{2,1,0:T(4,128)} async-done(((f32[32,4,5120]{2,1,0:T(4,128)}), f32[32,4,5120]{2,1,0:T(4,128)}) %all-reduce.6.cloned.1.call-update) | async-done | bytes 2621456
  372.4 19.7 %all-gather.1 = f32[16,2,32]{2,1,0:T(2,128)S(1)} all-gather(f32[1,2,32]{2,1,0:T(2,128)S(1)} %reshape.282), channel_id=1, replica_groups=mesh['parts'=2,'tp'=16] {'tp'}, dimensions={0}, use_global_device_ids=true | all-gather | bytes 4352 | tf_op jit(solution)/shard_map/all_gather | solution.py:179
  (103 shorter events, 22.3 us)
Async XLA Ops:
  7.2 364.7 %copy-start = (bf16[2,8,5120]{2,1,0:T(8,128)(2,1)S(1)}, bf16[2,8,5120]{2,1,0:T(8,128)(2,1)}, u32[]{:S(2)}) copy-start(bf16[2,8,5120]{2,1,0:T(8,128)(2,1)} %param.41) | copy-start | bytes 491524
  7.2 45.6 %copy-start.10 = (bf16[128]{0:T(256)(128)(2,1)S(1)}, bf16[128]{0:T(256)(128)(2,1)}, u32[]{:S(2)}) copy-start(bf16[128]{0:T(256)(128)(2,1)} %param.29) | copy-start | bytes 772
  7.2 45.7 %copy-start.11 = (bf16[128]{0:T(256)(128)(2,1)S(1)}, bf16[128]{0:T(256)(128)(2,1)}, u32[]{:S(2)}) copy-start(bf16[128]{0:T(256)(128)(2,1)} %param.28) | copy-start | bytes 772
  7.2 126.0 %all-reduce.4.cloned.1.call-start = ((), (), s32[]{:S(2)}) async-start(), calls=%async_computation.4 | async-start | bytes 196608 | tf_op jit(solution)/shard_map/psum | solution.py:126
  48.7 125.5 %all-gather.4.cloned.1.call-start = ((), (), s32[]{:S(2)}) async-start(), calls=%async_computation.3 | async-start | bytes 1392640 | tf_op jit(solution)/shard_map/all_gather | solution.py:138
  71.6 6.3 %copy-start.9 = (s32[2]{0:T(128)S(1)}, s32[2]{0:T(128)}, u32[]{:S(2)}) copy-start(s32[2]{0:T(128)} %param.40) | copy-start | bytes 28
  71.6 61.7 %copy-start.5 = (bf16[64,64]{1,0:T(8,128)(2,1)S(1)}, bf16[64,64]{1,0:T(8,128)(2,1)}, u32[]{:S(2)}) copy-start(bf16[64,64]{1,0:T(8,128)(2,1)} %param.35) | copy-start | bytes 24580
  71.6 62.7 %copy-start.6 = (bf16[64,64]{1,0:T(8,128)(2,1)S(1)}, bf16[64,64]{1,0:T(8,128)(2,1)}, u32[]{:S(2)}) copy-start(bf16[64,64]{1,0:T(8,128)(2,1)} %param.34) | copy-start | bytes 24580
  71.6 63.7 %copy-start.3 = (bf16[64,512]{1,0:T(8,128)(2,1)S(1)}, bf16[64,512]{1,0:T(8,128)(2,1)}, u32[]{:S(2)}) copy-start(bf16[64,512]{1,0:T(8,128)(2,1)} %param.33) | copy-start | bytes 196612
  179.2 12.0 %all-to-all-start.1 = ((bf16[32,4,640]{2,1,0:T(4,128)(2,1)}), bf16[32,4,640]{2,1,0:T(4,128)(2,1)S(1)}, u32[]{:S(2)}, u32[]{:S(2)}) async-start(bf16[32,4,640]{2,1,0:T(4,128)(2,1)} %reshape.271), calls=%async_computation.1 | async-start | bytes 327680 | tf_op jit(solution)/shard_map/all_to_all | solution.py:146
  202.4 17.8 %copy-start.4 = (bf16[64,320]{1,0:T(8,128)(2,1)S(1)}, bf16[64,320]{1,0:T(8,128)(2,1)}, u32[]{:S(2)}) copy-start(bf16[64,320]{1,0:T(8,128)(2,1)} %param.37) | copy-start | bytes 122884
  216.6 28.7 %all-to-all-start.2 = ((bf16[16,2,2048]{2,1,0:T(2,128)(2,1)}), bf16[16,2,2048]{2,1,0:T(2,128)(2,1)S(1)}, u32[]{:S(2)}, u32[]{:S(2)}) async-start(bf16[16,2,2048]{2,1,0:T(2,128)(2,1)} %reshape.288), calls=%async_computation.2 | async-start | bytes 262144 | tf_op jit(solution)/shard_map/all_to_all | solution.py:157
  220.1 150.7 %all-reduce.6.cloned.1.call-start = ((), (), s32[]{:S(2)}) async-start(), calls=%async_computation.5 | async-start | bytes 5242880
  265.1 3.4 copy-start.2
  270.0 5.5 %copy-start.8 = (s32[32,1]{0,1:T(1,128)S(1)}, s32[32,1]{0,1:T(1,128)}, u32[]{:S(2)}) copy-start(s32[32,1]{0,1:T(1,128)} %param.43) | copy-start | bytes 388
  270.0 5.9 %copy-start.7 = (bf16[5120]{0:T(1024)(128)(2,1)S(1)}, bf16[5120]{0:T(1024)(128)(2,1)}, u32[]{:S(2)}) copy-start(bf16[5120]{0:T(1024)(128)(2,1)} %param.42) | copy-start | bytes 30724
  270.0 5.9 %copy-start.12 = (u32[32]{0:T(128)S(1)}, u32[32]{0:T(128)}, u32[]{:S(2)}) copy-start(u32[32]{0:T(128)} %constant.48) | copy-start | bytes 388
  272.0 12.8 %all-to-all-start = ((bf16[32,4,320]{2,1,0:T(4,128)(2,1)}), bf16[32,4,320]{2,1,0:T(4,128)(2,1)S(1)}, u32[]{:S(2)}, u32[]{:S(2)}) async-start(bf16[32,4,320]{2,1,0:T(4,128)(2,1)} %param.22), calls=%async_computation | async-start | bytes 196608 | tf_op jit(solution)/shard_map/all_to_all | solution.py:169
  371.9 20.9 %copy-start.1 = (bf16[2,4,5120]{2,1,0:T(4,128)(2,1)}, bf16[2,4,5120]{2,1,0:T(4,128)(2,1)S(1)}, u32[]{:S(2)}) copy-start(bf16[2,4,5120]{2,1,0:T(4,128)(2,1)S(1)} %get-tuple-element.3) | copy-start | bytes 245764
Sparse Core Ops, SparseCore 0:
  48.8 84.4 all-reduce.3
  136.3 37.7 all-gather.3
  272.1 98.6 all-reduce.5
where the time goes:
time: 401 us; the launch traced here: 399 us
  waiting for transfers between devices  195 us (49%)
  blocking collectives  78.7 us (20%)
  local copies, waits for them, and re-layouts  68.2 us (17%)
  matrix products  25.9 us (6%)
  between operations  14.9 us (4%)
  starting transfers between devices  10.7 us (3%)
  other arithmetic  6.18 us (2%)
    unnamed x4, waiting for transfers between devices  86 us
    psum x1, waiting for transfers between devices, on_device(): low_full = lax.psum(partial_low, 'tp')  55 us
    all_gather x1, waiting for transfers between devices, on_device(): lax.all_gather(flat_normed, 'tp', axis=1, tiled=True)  37.8 us
    unnamed x36, local copies, waits for them, and re-layouts  36.6 us
    psum x1, blocking collectives, on_device(): squares = lax.psum(jnp.sum(x_float * x_float, axis=-1), 'tp')  34.9 us
    all_gather x1, blocking collectives, on_device(): up_full = lax.all_gather(b_out, 'tp', axis=1, tiled=True)  24.1 us
    all_gather x1, blocking collectives, on_device(): all_rows = lax.all_gather(logprob, 'tp', axis=0, tiled=True)  19.7 us
    all_to_all x1, local copies, waits for them, and re-layouts, on_device(): lax.all_to_all(attended, 'tp', split_axis=2, concat_axis=0, tiled=True)  9.68 us
  transfers between devices with their start and end apart: 6, of which 5 were waited for; matrix products, arithmetic and copies ran while one was open for 9% of the time, Pallas kernels for 0%

commit v1 on v0

--- a/solution.py
+++ b/solution.py
@@ -2,7 +2,10 @@
 
 import jax
 import jax.numpy as jnp
+import numpy as np
 from jax import lax
+from jax.experimental import pallas as pl
+from jax.experimental.pallas import tpu as pltpu
 from jax.sharding import PartitionSpec as P
 
 CAP = 4
@@ -183,6 +186,470 @@
     return (hidden_out, cand_logprob)
 
 
+MESH = pl.DeviceIdType.MESH
+NZ, NY, NC = 4, 2, 2
+FUSED_TP = NZ * NY * NC
+CHUNKS = 4
+F32, BF16 = jnp.float32, jnp.bfloat16
+
+
+def dot_nt(left, right):
+    return lax.dot_general(left, right, (((1,), (1,)), ((), ())), preferred_element_type=F32)
+
+
+def dot_nn(left, right):
+    return jnp.dot(left, right, preferred_element_type=F32)
+
+
+def split_high_low(values):
+    high = values.astype(BF16)
+    return high, (values - high.astype(F32)).astype(BF16)
+
+
+def fused_kernel(
+    x_ref, gain_ref, wq_hbm, wk_hbm, wv_hbm, wo_hbm, qg_ref, kg_ref, aq_ref, ak_ref, av_ref,
+    bq_ref, bk_ref, bv_ref, ao_ref, bo_ref, kc_hbm, vc_hbm, len_ref, cand_ref, fg_ref, freq_ref,
+    pick_ref,
+    hid_ref, lp_ref,
+    wq, wkv, wo, keys, vals, xall, ball, lowp, lowr, lowall, upm, accq, acckv, xres, bfull,
+    projs, projr, atts, attr, parts, got_c, half_y, got_y, quarter, got_z, hidden, lpall,
+    local_sem, xs, xr, bs, br, l1s, l1r, l2s, l2r, ps, pr, ats, atr,
+    cs, cr, ys, yr, zs, zr, gs, gr,
+):
+    n = FUSED_TP
+    me = lax.axis_index("tp")
+    core, y, z = lax.rem(me, NC), lax.rem(me // NC, NY), me // (NC * NY)
+    groups, rows8, part = x_ref.shape
+    width = part * n
+    rank = aq_ref.shape[0]
+    span = kc_hbm.shape[1]
+    padded = keys.shape[1]
+    head = qg_ref.shape[1]
+    qcols = wq.shape[1]
+    rows = groups * rows8
+    chunk = width // CHUNKS
+
+    def place(pz, py, pc):
+        return (pz * NY + py) * NC + pc
+
+    y_peer, c_peer = place(z, 1 - y, core), place(z, y, 1 - core)
+
+    def remote(source, target, send, recv, device):
+        return pltpu.make_async_remote_copy(
+            src_ref=source, dst_ref=target, send_sem=send, recv_sem=recv,
+            device_id={"tp": device}, device_id_type=MESH,
+        )
+
+    loads = [
+        pltpu.make_async_copy(wq_hbm, wq, local_sem.at[0]),
+        pltpu.make_async_copy(wk_hbm, wkv.at[pl.ds(0, wk_hbm.shape[0])], local_sem.at[1]),
+        pltpu.make_async_copy(wv_hbm, wkv.at[pl.ds(wk_hbm.shape[0], wk_hbm.shape[0])], local_sem.at[2]),
+        pltpu.make_async_copy(kc_hbm.at[0], keys.at[0, pl.ds(0, span)], local_sem.at[3]),
+        pltpu.make_async_copy(kc_hbm.at[1], keys.at[1, pl.ds(0, span)], local_sem.at[4]),
+        pltpu.make_async_copy(vc_hbm.at[0], vals.at[0, pl.ds(0, span)], local_sem.at[5]),
+        pltpu.make_async_copy(vc_hbm.at[1], vals.at[1, pl.ds(0, span)], local_sem.at[6]),
+        pltpu.make_async_copy(wo_hbm, wo, local_sem.at[7]),
+    ]
+    for load in loads:
+        load.start()
+
+    barrier = pltpu.get_barrier_semaphore()
+
+    def greet(d, carry):
+        pl.semaphore_signal(barrier, inc=1, device_id={"tp": lax.rem(me + d, n)}, device_id_type=MESH)
+        return carry
+
+    lax.fori_loop(1, n, greet, 0)
+
+    xall[me, 0:groups] = x_ref[...]
+    xall[me, groups] = jnp.broadcast_to(gain_ref[...].astype(F32), (rows8, part)).astype(BF16)
+    ball[me] = bo_ref[...]
+    pl.semaphore_wait(barrier, n - 1)
+
+    def gather(buffer, send, recv):
+        def hop(block, device, number):
+            return remote(buffer.at[block], buffer.at[block], send.at[number], recv.at[block], device)
+
+        def begin():
+            hop(me, y_peer, 0).start()
+            for dz in range(1, NZ):
+                hop(me, place(lax.rem(z + dz, NZ), y, core), dz).start()
+            hop(me, c_peer, NZ).start()
+
+        def middle():
+            for dz in range(1, NZ):
+                block = place(lax.rem(z + dz, NZ), y, core)
+                hop(block, y_peer, 0).wait_recv()
+                hop(block, y_peer, NZ + dz).start()
+                hop(block, c_peer, 2 * NZ - 1 + dz).start()
+
+        def late():
+            for dz in range(NZ):
+                block = place(lax.rem(z + dz, NZ), 1 - y, core)
+                hop(block, c_peer, 0).wait_recv()
+                hop(block, c_peer, 3 * NZ - 1 + dz).start()
+
+        def finish():
+            for dz in range(NZ):
+                for py in range(NY):
+                    hop(place(lax.rem(z + dz, NZ), py, 1 - core), c_peer, 0).wait_recv()
+
+        def drain():
+            for number in range(n - 1):
+                hop(me, c_peer, number).wait_send()
+
+        return begin, middle, late, finish, drain
+
+    def exchange(source, target, send, recv, spread):
+        def copy(to, slot, device):
+            part_of = source.at[me] if spread else source.at[to]
+            return remote(part_of, target.at[slot], send.at[to], recv.at[slot], device)
+
+        def begin():
+            def one(d, carry):
+                to = lax.rem(me + d, n)
+                copy(to, me, to).start()
+                return carry
+
+            lax.fori_loop(1, n, one, 0)
+
+        def finish():
+            def one(d, carry):
+                other = lax.rem(me + d, n)
+                copy(other, other, other).wait_recv()
+                return carry
+
+            lax.fori_loop(1, n, one, 0)
+
+        def drain():
+            def one(d, carry):
+                other = lax.rem(me + d, n)
+                copy(other, other, other).wait_send()
+                return carry
+
+            lax.fori_loop(1, n, one, 0)
+
+        return begin, finish, drain
+
+    x_gather = gather(xall, xs, xr)
+    b_gather = gather(ball, bs, br)
+    low_scatter = exchange(lowp, lowr, l1s, l1r, False)
+    low_spread = exchange(lowall, lowall, l2s, l2r, True)
+    proj_swap = exchange(projs, projr, ps, pr, False)
+    att_swap = exchange(atts, attr, ats, atr, False)
+    lp_spread = exchange(lpall, lpall, gs, gr, True)
+
+    x_gather[0]()
+
+    own = x_ref[...].astype(F32).reshape(rows, part)
+    own_gained = (own * gain_ref[...].astype(F32)).astype(BF16)
+    down = jnp.concatenate([aq_ref[...], ak_ref[...], av_ref[...], jnp.zeros((rank, part), BF16)], axis=0)
+    low_part = dot_nt(own_gained, down)
+    square = jnp.sum(own * own, axis=-1, keepdims=True)
+    lane = lax.broadcasted_iota(jnp.int32, low_part.shape, 1)
+    lowp[...] = jnp.where(lane < 3 * rank, low_part, square).reshape(lowp.shape)
+    lowr[me] = lowp[me]
+    low_scatter[0]()
+
+    upm[...] = jnp.zeros_like(upm)
+    upm[0:rank, 0:qcols] = bq_ref[...]
+    empty = jnp.zeros(bk_ref.shape, F32)
+    upm[rank : 2 * rank, qcols:] = jnp.concatenate([bk_ref[...].astype(F32), empty], axis=1).astype(BF16)
+    upm[2 * rank : 3 * rank, qcols:] = jnp.concatenate([empty, bv_ref[...].astype(F32)], axis=1).astype(BF16)
+    for r in range(2):
+        keys[r, span:padded] = jnp.zeros((padded - span, keys.shape[2]), BF16)
+        vals[r, span:padded] = jnp.zeros((padded - span, vals.shape[2]), BF16)
+    sub8 = lax.broadcasted_iota(jnp.int32, (rows8, head), 0)
+    lane8 = lax.broadcasted_iota(jnp.int32, (rows8, head), 1)
+    steps = rows8 // 2
+    position = jnp.where(sub8 < steps, len_ref[0] + sub8, len_ref[1] + sub8 - steps).astype(F32)
+    angle = position * freq_ref[...]
+    cosine = jnp.cos(angle)[None]
+    sine = jnp.sin(angle)
+    sine = jnp.where(lane8 < head // 2, -sine, sine)[None]
+
+    x_gather[1]()
+    low_scatter[1]()
+    lowall[me] = jnp.sum(lowr[...], axis=0)
+    low_spread[0]()
+    x_gather[2]()
+    for load in loads[:3]:
+        load.wait()
+    x_gather[3]()
+    b_gather[0]()
+
+    pair = NC * part
+    for m in range(n // 2):
+        sides, kept = [], []
+        for b in (2 * m, 2 * m + 1):
+            block = xall[b, 0:groups].astype(F32).reshape(rows, part)
+            sides.append(block * xall[b, groups].astype(F32)[0:1])
+            kept.append(xall[b, me].astype(F32))
+        gained = jnp.concatenate(sides, axis=1).astype(BF16)
+        xres[:, m * pair : (m + 1) * pair] = jnp.concatenate(kept, axis=1)
+        more_q = dot_nn(gained, wq[m * pair : (m + 1) * pair, :])
+        more_kv = dot_nt(gained, wkv[:, m * pair : (m + 1) * pair])
+        accq[...] = more_q if m == 0 else accq[...] + more_q
+        acckv[...] = more_kv if m == 0 else acckv[...] + more_kv
+
+    low_spread[1]()
+    low_all = lowall[...].reshape(rows, lowall.shape[2])
+    inverse = lax.rsqrt(low_all[:, 3 * rank : 3 * rank + 1] / width + EPSILON)
+    low_high, low_low = split_high_low(jnp.where(lane < 3 * rank, low_all * inverse, 0.0))
+    lifted = dot_nn(low_high, upm[...]) + dot_nn(low_low, upm[...])
+    projs[:, :, 0:qcols] = (accq[...] * inverse + lifted[:, 0:qcols]).reshape(groups, rows8, qcols).astype(BF16)
+    projs[:, :, qcols:] = (acckv[...] * inverse + lifted[:, qcols:]).reshape(groups, rows8, head).astype(BF16)
+    projr[me] = projs[me]
+    proj_swap[0]()
+    b_gather[1]()
+    proj_swap[1]()
+    b_gather[2]()
+
+    def normed_heads(values, gain_row):
+        scaled = values * lax.rsqrt(jnp.mean(values * values, axis=-1, keepdims=True) + EPSILON)
+        scaled = scaled * gain_row[...].astype(F32)[None]
+        return scaled * cosine + pltpu.roll(scaled, head // 2, 2) * sine
+
+    sub16 = lax.broadcasted_iota(jnp.int32, (n, rows8, head), 1)
+    by_row = [[], []]
+    for p in range(qcols // (2 * head)):
+        first = normed_heads(projr[:, :, 2 * p * head : (2 * p + 1) * head].astype(F32), qg_ref)
+        second = normed_heads(projr[:, :, (2 * p + 1) * head : (2 * p + 2) * head].astype(F32), qg_ref)
+        by_row[0].append(jnp.where(sub16 < steps, first, pltpu.roll(second, steps, 1)))
+        by_row[1].append(jnp.where(sub16 < steps, pltpu.roll(first, steps, 1), second))
+    kv_groups = n // 2
+    kv_all = projr[:, :, qcols:].astype(F32).reshape(kv_groups, 2, rows8, head)
+    even, odd = kv_all[:, 0], kv_all[:, 1]
+    lane_kv = lax.broadcasted_iota(jnp.int32, even.shape, 2)
+    new_keys = normed_heads(jnp.where(lane_kv < head // 2, even, pltpu.roll(odd, head // 2, 2)), kg_ref)
+    new_vals = jnp.where(lane_kv < head // 2, pltpu.roll(even, head // 2, 2), odd)
+
+    for load in loads[3:7]:
+        load.wait()
+    blank = jnp.zeros((rows8, head), F32)
+    for g in range(kv_groups):
+        new_key = jnp.concatenate([new_keys[g], blank], axis=0).astype(BF16)
+        new_val = jnp.concatenate([new_vals[g], blank], axis=0).astype(BF16)
+        for r in range(2):
+            keys[r, span : span + 2 * rows8, g * head : (g + 1) * head] = new_key
+            vals[r, span : span + 2 * rows8, g * head : (g + 1) * head] = new_val
+
+    asked = 4 * rows8
+    column = lax.broadcasted_iota(jnp.int32, (asked, padded), 1)
+    step_of = lax.rem(lax.broadcasted_iota(jnp.int32, (asked, padded), 0), steps)
+    live = []
+    for r in range(2):
+        fresh = column - span - r * steps
+        in_cache = (column < len_ref[r]) & (column < span)
+        live.append((in_cache | ((fresh >= 0) & (fresh <= step_of) & (column >= span))).astype(F32))
+    sub4 = lax.broadcasted_iota(jnp.int32, (4, rows8, head), 1)
+    for g in range(kv_groups):
+        outs = []
+        for r in range(2):
+            tiles = [by_row[r][p][2 * g + side][None] for side in range(2) for p in range(2)]
+            query = jnp.concatenate(tiles, axis=0).reshape(asked, head).astype(BF16)
+            scores = dot_nt(query, keys[r, :, g * head : (g + 1) * head]) * (1.0 / math.sqrt(head))
+            weights = jnp.exp(scores) * live[r]
+            total = jnp.sum(weights, axis=-1, keepdims=True)
+            mixed = dot_nn(weights.astype(BF16), vals[r, :, g * head : (g + 1) * head]) / total
+            outs.append(mixed.reshape(4, rows8, head))
+        first = jnp.where(sub4 < steps, outs[0], pltpu.roll(outs[1], steps, 1)).astype(BF16)
+        second = jnp.where(sub4 < steps, pltpu.roll(outs[0], steps, 1), outs[1]).astype(BF16)
+        for side in range(2):
+            for p in range(2):
+                atts[2 * g + side, :, 2 * p * head : (2 * p + 1) * head] = first[2 * side + p]
+                atts[2 * g + side, :, (2 * p + 1) * head : (2 * p + 2) * head] = second[2 * side + p]
+    attr[me] = atts[me]
+    att_swap[0]()
+    b_gather[3]()
+    for m in range(n // 2):
+        bfull[:, m * pair : (m + 1) * pair] = jnp.concatenate(
+            [ball[2 * m].astype(F32), ball[2 * m + 1].astype(F32)], axis=1
+        ).astype(BF16)
+    loads[7].wait()
+    att_swap[1]()
+
+    segment = attr[...].astype(F32).reshape(rows, qcols).astype(BF16)
+    inner_high, inner_low = split_high_low(dot_nt(segment, ao_ref[...]))
+
+    def c_hop(k):
+        return remote(parts.at[k, 1 - core], got_c.at[k], cs.at[k], cr.at[k], c_peer)
+
+    def y_hop(k):
+        return remote(half_y.at[k, 1 - y], got_y.at[k], ys.at[k], yr.at[k], y_peer)
+
+    def z_hop(k, dz):
+        other = lax.rem(z + dz, NZ)
+        return remote(quarter.at[k, other], got_z.at[k, dz - 1], zs.at[k, dz - 1], zr.at[k, dz - 1], place(other, y, core))
+
+    def multiply(k):
+        at = slice(k * chunk, (k + 1) * chunk)
+        up = bfull[:, at]
+        out = dot_nn(segment, wo[:, at]) + (dot_nn(inner_high, up) + dot_nn(inner_low, up))
+        out = out.reshape(groups // NC, NC, rows8, chunk).astype(BF16)
+        for pc in range(NC):
+            parts[k, pc] = out[:, pc]
+        c_hop(k).start()
+
+    def over_y(k):
+        c_hop(k).wait_recv()
+        both = parts[k, core].astype(F32) + got_c[k].astype(F32)
+        both = both.reshape(NZ, NY, rows8, chunk).astype(BF16)
+        for py in range(NY):
+            half_y[k, py] = both[:, py]
+        y_hop(k).start()
+
+    def over_z(k):
+        y_hop(k).wait_recv()
+        quarter[k] = (half_y[k, y].astype(F32) + got_y[k].astype(F32)).astype(BF16)
+        for dz in range(1, NZ):
+            z_hop(k, dz).start()
+
+    for k in range(CHUNKS):
+        multiply(k)
+        if k >= 1:
+            over_y(k - 1)
+    over_y(CHUNKS - 1)
+    for k in range(CHUNKS):
+        over_z(k)
+
+    squares = jnp.zeros((rows8, 1), F32)
+    for k in range(CHUNKS):
+        at = slice(k * chunk, (k + 1) * chunk)
+        total = xres[:, at] + quarter[k, z].astype(F32)
+        for dz in range(1, NZ):
+            z_hop(k, dz).wait_recv()
+            total = total + got_z[k, dz - 1].astype(F32)
+        rounded = total.astype(BF16)
+        hid_ref[:, at] = rounded
+        rounded = rounded.astype(F32)
+        hidden[:, at] = rounded
+        squares = squares + jnp.sum(rounded * rounded, axis=-1, keepdims=True)
+    final = (hidden[...] * lax.rsqrt(squares / width + EPSILON) * fg_ref[...].astype(F32)).astype(BF16)
+    cands = cand_ref.shape[1]
+    logits = jnp.where(
+        lax.broadcasted_iota(jnp.int32, (rows8, cands), 0) < steps,
+        dot_nt(final, cand_ref[0]),
+        dot_nt(final, cand_ref[1]),
+    )
+    logprob = logits - jnp.log(jnp.sum(jnp.exp(logits), axis=-1, keepdims=True))
+    lpall[me] = jnp.concatenate([logprob, jnp.zeros((rows8, lpall.shape[2] - cands), F32)], axis=1)
+    lp_spread[0]()
+    lp_spread[1]()
+    placed = jnp.dot(
+        pick_ref[...], lpall[...].reshape(rows, lpall.shape[2]),
+        precision=lax.Precision.HIGHEST, preferred_element_type=F32,
+    )
+    lp_ref[...] = placed[:, 0:cands]
+
+    x_gather[4]()
+    b_gather[4]()
+    for swap in (low_scatter, low_spread, proj_swap, att_swap, lp_spread):
+        swap[2]()
+    for k in range(CHUNKS):
+        c_hop(k).wait_send()
+        y_hop(k).wait_send()
+        for dz in range(1, NZ):
+            z_hop(k, dz).wait_send()
+
+
+def fused_on_device(
+    x_in, ln_gain, w_query, w_key, w_value, w_out, q_gain, k_gain, a_query, a_key, a_value,
+    b_query, b_key, b_value, a_out, b_out, key_cache, value_cache, kv_length, cand_rows,
+    final_gain, row_owner,
+):
+    n = lax.axis_size("tp")
+    me = lax.axis_index("tp")
+    row_count, step_count, part = x_in.shape
+    rows8 = row_count * step_count // n
+    width = part * n
+    head = q_gain.shape[0]
+    qcols = w_query.shape[1]
+    kvcols = w_key.shape[1]
+    cols = qcols + 2 * kvcols
+    rank = a_query.shape[1]
+    span, kv_width = key_cache.shape[1:]
+    cands = cand_rows.shape[1]
+    half = head // 2
+    frequency = ROPE_BASE ** (-np.arange(half, dtype=np.float32) / np.float32(half))
+    frequency = jnp.asarray(np.concatenate([frequency, frequency])[None, :].astype(np.float32))
+
+    slot_index = slot_of(row_owner[:, 0], n, CAP)
+    wanted = me * CAP + jnp.arange(CAP, dtype=jnp.int32)
+    select = (slot_index[None, :] == wanted[:, None]).astype(F32)
+    same_step = jnp.eye(step_count, dtype=F32)
+    pick = (select[:, None, :, None] * same_step[None, :, None, :]).reshape(
+        CAP * step_count, row_count * step_count
+    )
+
+    chunk = width // CHUNKS
+    rows = row_count * step_count
+    padded = span + 128
+    vmem = pl.BlockSpec(memory_space=pltpu.VMEM)
+    smem = pl.BlockSpec(memory_space=pltpu.SMEM)
+    hbm = pl.BlockSpec(memory_space=pl.ANY)
+    dma = pltpu.SemaphoreType.DMA
+    hidden_out, cand_logprob = pl.pallas_call(
+        fused_kernel,
+        out_shape=(
+            jax.ShapeDtypeStruct((rows8, width), BF16),
+            jax.ShapeDtypeStruct((CAP * step_count, cands), F32),
+        ),
+        in_specs=[vmem, vmem, hbm, hbm, hbm, hbm, vmem, vmem, vmem, vmem, vmem,
+                  vmem, vmem, vmem, vmem, vmem, hbm, hbm, smem, vmem, vmem, vmem, vmem],
+        out_specs=(vmem, vmem),
+        scratch_shapes=[
+            pltpu.VMEM((width, qcols), BF16),
+            pltpu.VMEM((2 * kvcols, width), BF16),
+            pltpu.VMEM((qcols, width), BF16),
+            pltpu.VMEM((2, padded, kv_width), BF16),
+            pltpu.VMEM((2, padded, kv_width), BF16),
+            pltpu.VMEM((n, n + 1, rows8, part), BF16),
+            pltpu.VMEM((n, rank, part), BF16),
+            pltpu.VMEM((n, rows8, 4 * rank), F32),
+            pltpu.VMEM((n, rows8, 4 * rank), F32),
+            pltpu.VMEM((n, rows8, 4 * rank), F32),
+            pltpu.VMEM((4 * rank, cols), BF16),
+            pltpu.VMEM((rows, qcols), F32),
+            pltpu.VMEM((rows, 2 * kvcols), F32),
+            pltpu.VMEM((rows8, width), F32),
+            pltpu.VMEM((rank, width), BF16),
+            pltpu.VMEM((n, rows8, cols), BF16),
+            pltpu.VMEM((n, rows8, cols), BF16),
+            pltpu.VMEM((n, rows8, qcols), BF16),
+            pltpu.VMEM((n, rows8, qcols), BF16),
+            pltpu.VMEM((CHUNKS, NC, NZ * NY, rows8, chunk), BF16),
+            pltpu.VMEM((CHUNKS, NZ * NY, rows8, chunk), BF16),
+            pltpu.VMEM((CHUNKS, NY, NZ, rows8, chunk), BF16),
+            pltpu.VMEM((CHUNKS, NZ, rows8, chunk), BF16),
+            pltpu.VMEM((CHUNKS, NZ, rows8, chunk), BF16),
+            pltpu.VMEM((CHUNKS, NZ - 1, rows8, chunk), BF16),
+            pltpu.VMEM((rows8, width), F32),
+            pltpu.VMEM((n, rows8, 128), F32),
+            dma((8,)),
+            dma((n,)), dma((n,)), dma((n,)), dma((n,)),
+            dma((n,)), dma((n,)), dma((n,)), dma((n,)),
+            dma((n,)), dma((n,)), dma((n,)), dma((n,)),
+            dma((CHUNKS,)), dma((CHUNKS,)), dma((CHUNKS,)), dma((CHUNKS,)),
+            dma((CHUNKS, NZ - 1)), dma((CHUNKS, NZ - 1)),
+            dma((n,)), dma((n,)),
+        ],
+        compiler_params=pltpu.CompilerParams(
+            collective_id=0, has_side_effects=True, vmem_limit_bytes=56 * 1024 * 1024
+        ),
+        name="layer",
+    )(
+        x_in.reshape(n, rows8, part), ln_gain[None, :], w_query, w_key.T, w_value.T, w_out,
+        q_gain[None, :], k_gain[None, :], a_query.T, a_key.T, a_value.T, b_query, b_key, b_value,
+        a_out.T, b_out, key_cache, value_cache, kv_length, cand_rows, final_gain[None, :],
+        frequency, pick,
+    )
+    return (
+        hidden_out.reshape(row_count // n, step_count, width),
+        cand_logprob.reshape(CAP, step_count * cands),
+    )
+
+
 def solution(mesh):
     placed = (
         P("parts", None, "tp"),
@@ -209,7 +676,7 @@
         P("parts", None),
     )
     return jax.shard_map(
-        on_device,
+        fused_on_device if mesh.shape["tp"] == FUSED_TP else on_device,
         mesh=mesh,
         in_specs=placed,
         out_specs=(P(("parts", "tp"), None, None), P(("parts", "tp"), None)),

time: 401 us -> 82.9 us (0.21)
  waiting for transfers between devices: 195 us -> 0 us
  blocking collectives: 78.7 us -> 0 us
  Pallas kernels: 0 us -> 71.7 us
  local copies, waits for them, and re-layouts: 68.2 us -> 7.8 us
  matrix products: 25.9 us -> 0 us
  between operations: 14.9 us -> 0.65 us
  starting transfers between devices: 10.7 us -> 0 us
    unnamed x4 -> x0, waiting for transfers between devices: 86 us -> none
    pallas_call x0 -> x1, Pallas kernels: none -> 71.7 us  [fused_on_device(): pl.pallas_call(fused_kernel, out_shape=(jax.ShapeDtypeStruct((rows8, widt...]
    psum x1 -> x0, waiting for transfers between devices: 55 us -> none  [on_device(): low_full = lax.psum(partial_low, 'tp')]
    all_gather x2 -> x0, blocking collectives: 43.7 us -> none  [the longest x1 24.1 us: on_device(): up_full = lax.all_gather(b_out, 'tp', axis=1, tiled=True)]
    all_gather x1 -> x0, waiting for transfers between devices: 37.8 us -> none  [on_device(): lax.all_gather(flat_normed, 'tp', axis=1, tiled=True)]
    unnamed x36 -> x0, local copies, waits for them, and re-layouts: 36.6 us -> none
    psum x1 -> x0, blocking collectives: 34.9 us -> none  [on_device(): squares = lax.psum(jnp.sum(x_float * x_float, axis=-1), 'tp')]
    dot_general x14 -> x0, matrix products: 25.9 us -> none  [the longest x1 5.23 us: attend(): jnp.einsum('rsngd,rtnd->rsngt', grouped, key_all, preferred_element_type=...]
  transfers between devices with their start and end apart: 6 -> 0, of which waited for: 5 -> 0; matrix products, arithmetic and copies ran while one was open for 9% -> 0% of each run, Pallas kernels for 0% -> 0%
where the time goes in v1:
time: 82.9 us; the launch traced here: 82.6 us
  Pallas kernels  71.7 us (86%)
  local copies, waits for them, and re-layouts  7.8 us (9%)
  other arithmetic  2.45 us (3%)
    pallas_call x1, Pallas kernels, fused_on_device(): pl.pallas_call(fused_kernel, out_shape=(jax.ShapeDtypeStruct((rows8, widt...  71.7 us

profile of v1, /device:TPU:0, one launch (start us, length us, event | category | flops | bytes accessed | tf_op | source)
XLA Modules:
  0.0 82.6 jit_solution(15816462553035456373)
XLA Ops:
  0.6 0.7 fusion
  1.4 0.1 reduce_window_sum.11
  1.4 0.8 %select_reduce_fusion = s32[32]{0:T(128)S(1)} fusion(s32[32,16]{1,0:T(8,128)S(1)} %reduce_window_sum.11, s32[32]{0:T(128)} %bitcast.19), kind=kLoop, calls=%fused_computation.1 | loop fusion | flops 2528 | bytes 2304 | tf_op jit(solution)/shard_map/reduce_sum | solution.py:51
  2.2 0.7 multiply_add_fusion
  2.9 0.1 compare_convert_fusion
  3.0 0.1 broadcast_multiply_fusion
  3.1 0.8 mul.40.pick_ref
  3.9 1.6 %reshape.64.x_ref = bf16[16,8,320]{2,1,0:T(8,128)(2,1)} reshape(bf16[32,4,320]{2,1,0:T(4,128)(2,1)} %param.23) | data formatting | bytes 163840 | tf_op jit(solution)/shard_map/reshape | solution.py:642
  5.4 1.3 %broadcast_in_dim.20.fg_ref = bf16[1,5120]{1,0:T(2,128)(2,1)} reshape(bf16[5120]{0:T(1024)(128)(2,1)} %param.43) | data formatting | bytes 20480 | tf_op jit(solution)/shard_map/broadcast_in_dim | solution.py:644
  6.7 1.2 %broadcast_in_dim.8.gain_ref = bf16[1,320]{1,0:T(2,128)(2,1)} reshape(bf16[320]{0:T(512)(128)(2,1)} %param.24) | data formatting | bytes 1280 | tf_op jit(solution)/shard_map/broadcast_in_dim | solution.py:642
  8.0 71.7 %layer.1 = (bf16[8,5120]{1,0:T(8,128)(2,1)}, f32[16,8]{1,0:T(8,128)}) custom-call(bf16[16,8,320]{2,1,0:T(8,128)(2,1)} %reshape.64.x_ref, bf16[1,320]{1,0:T(2,128)(2,1)} %broadcast_in_dim.8.gain_ref, bf16[5120,512]{1,0:T(8,128)(2,1)} %wq_hbm.1, bf16[64,5120]{1,0:T(8,128)(2,1)} %bitcast.12, bf16[64,5120]{1,0:T(8,128)(2,1)} %bitcast.13, ...), custom_call_target="tpu_custom_call" | custom-call | tf_op jit(solution)/shard_map/layer/pallas_call | solution.py:592
  79.7 1.6 %reshape.65 = bf16[2,4,5120]{2,1,0:T(4,128)(2,1)} reshape(bf16[8,5120]{1,0:T(8,128)(2,1)} %get-tuple-element.4) | data formatting | bytes 163840 | tf_op jit(solution)/shard_map/reshape | solution.py:648
  81.2 1.4 %reshape.66 = f32[4,32]{1,0:T(4,128)} reshape(f32[16,8]{1,0:T(8,128)} %get-tuple-element.5) | data formatting | bytes 1024 | tf_op jit(solution)/shard_map/reshape | solution.py:649
  (2 shorter events, 0.0 us)

commit v2 on v1

--- a/solution.py
+++ b/solution.py
@@ -208,18 +208,19 @@
 
 def fused_kernel(
     x_ref, gain_ref, wq_hbm, wk_hbm, wv_hbm, wo_hbm, qg_ref, kg_ref, aq_ref, ak_ref, av_ref,
-    bq_ref, bk_ref, bv_ref, ao_ref, bo_ref, kc_hbm, vc_hbm, len_ref, cand_ref, fg_ref, freq_ref,
-    pick_ref,
+    bq_hbm, bk_ref, bv_ref, ao_hbm, bo_ref, kc_hbm, vc_hbm, len_ref, cand_hbm, fg_ref, freq_ref,
+    owner_ref,
     hid_ref, lp_ref,
     wq, wkv, wo, keys, vals, xall, ball, lowp, lowr, lowall, upm, accq, acckv, xres, bfull,
-    projs, projr, atts, attr, parts, got_c, half_y, got_y, quarter, got_z, hidden, lpall,
+    bq_ref, ao_ref, cand_ref, pick, projs, projr, atts, attr, parts, got_c, half_y, got_y, quarter, got_z, hidden, lpall,
     local_sem, xs, xr, bs, br, l1s, l1r, l2s, l2r, ps, pr, ats, atr,
     cs, cr, ys, yr, zs, zr, gs, gr,
 ):
     n = FUSED_TP
     me = lax.axis_index("tp")
     core, y, z = lax.rem(me, NC), lax.rem(me // NC, NY), me // (NC * NY)
-    groups, rows8, part = x_ref.shape
+    row_count, steps, part = x_ref.shape
+    groups, rows8 = n, row_count * steps // n
     width = part * n
     rank = aq_ref.shape[0]
     span = kc_hbm.shape[1]
@@ -249,6 +250,9 @@
         pltpu.make_async_copy(vc_hbm.at[0], vals.at[0, pl.ds(0, span)], local_sem.at[5]),
         pltpu.make_async_copy(vc_hbm.at[1], vals.at[1, pl.ds(0, span)], local_sem.at[6]),
         pltpu.make_async_copy(wo_hbm, wo, local_sem.at[7]),
+        pltpu.make_async_copy(bq_hbm, bq_ref, local_sem.at[8]),
+        pltpu.make_async_copy(ao_hbm, ao_ref, local_sem.at[9]),
+        pltpu.make_async_copy(cand_hbm, cand_ref, local_sem.at[10]),
     ]
     for load in loads:
         load.start()
@@ -261,8 +265,10 @@
 
     lax.fori_loop(1, n, greet, 0)
 
-    xall[me, 0:groups] = x_ref[...]
-    xall[me, groups] = jnp.broadcast_to(gain_ref[...].astype(F32), (rows8, part)).astype(BF16)
+    own = x_ref[...].astype(F32).reshape(rows, part)
+    gain_row = gain_ref[...].astype(F32)[None, :]
+    xall[me, 0:groups] = own.reshape(groups, rows8, part).astype(BF16)
+    xall[me, groups] = jnp.broadcast_to(gain_row, (rows8, part)).astype(BF16)
     ball[me] = bo_ref[...]
     pl.semaphore_wait(barrier, n - 1)
 
@@ -341,8 +347,7 @@
 
     x_gather[0]()
 
-    own = x_ref[...].astype(F32).reshape(rows, part)
-    own_gained = (own * gain_ref[...].astype(F32)).astype(BF16)
+    own_gained = (own * gain_row).astype(BF16)
     down = jnp.concatenate([aq_ref[...], ak_ref[...], av_ref[...], jnp.zeros((rank, part), BF16)], axis=0)
     low_part = dot_nt(own_gained, down)
     square = jnp.sum(own * own, axis=-1, keepdims=True)
@@ -351,6 +356,7 @@
     lowr[me] = lowp[me]
     low_scatter[0]()
 
+    loads[8].wait()
     upm[...] = jnp.zeros_like(upm)
     upm[0:rank, 0:qcols] = bq_ref[...]
     empty = jnp.zeros(bk_ref.shape, F32)
@@ -361,12 +367,21 @@
         vals[r, span:padded] = jnp.zeros((padded - span, vals.shape[2]), BF16)
     sub8 = lax.broadcasted_iota(jnp.int32, (rows8, head), 0)
     lane8 = lax.broadcasted_iota(jnp.int32, (rows8, head), 1)
-    steps = rows8 // 2
     position = jnp.where(sub8 < steps, len_ref[0] + sub8, len_ref[1] + sub8 - steps).astype(F32)
     angle = position * freq_ref[...]
     cosine = jnp.cos(angle)[None]
     sine = jnp.sin(angle)
     sine = jnp.where(lane8 < head // 2, -sine, sine)[None]
+
+    sub_pick = lax.broadcasted_iota(jnp.int32, pick.shape, 0)
+    row_pick = lax.broadcasted_iota(jnp.int32, pick.shape, 1) // steps
+    chosen = jnp.zeros(pick.shape, F32)
+    owned = jnp.int32(0)
+    for row in range(row_count):
+        mine = (owner_ref[row] == me).astype(jnp.int32)
+        chosen = chosen + jnp.where((sub_pick == owned) & (row_pick == row), mine, 0).astype(F32)
+        owned = owned + mine
+    pick[...] = chosen
 
     x_gather[1]()
     low_scatter[1]()
@@ -401,9 +416,8 @@
     projs[:, :, qcols:] = (acckv[...] * inverse + lifted[:, qcols:]).reshape(groups, rows8, head).astype(BF16)
     projr[me] = projs[me]
     proj_swap[0]()
+    proj_swap[1]()
     b_gather[1]()
-    proj_swap[1]()
-    b_gather[2]()
 
     def normed_heads(values, gain_row):
         scaled = values * lax.rsqrt(jnp.mean(values * values, axis=-1, keepdims=True) + EPSILON)
@@ -461,12 +475,14 @@
                 atts[2 * g + side, :, (2 * p + 1) * head : (2 * p + 2) * head] = second[2 * side + p]
     attr[me] = atts[me]
     att_swap[0]()
+    b_gather[2]()
     b_gather[3]()
     for m in range(n // 2):
         bfull[:, m * pair : (m + 1) * pair] = jnp.concatenate(
             [ball[2 * m].astype(F32), ball[2 * m + 1].astype(F32)], axis=1
         ).astype(BF16)
-    loads[7].wait()
+    for load in (loads[7], loads[9], loads[10]):
+        load.wait()
     att_swap[1]()
 
     segment = attr[...].astype(F32).reshape(rows, qcols).astype(BF16)
@@ -521,11 +537,12 @@
             z_hop(k, dz).wait_recv()
             total = total + got_z[k, dz - 1].astype(F32)
         rounded = total.astype(BF16)
-        hid_ref[:, at] = rounded
         rounded = rounded.astype(F32)
+        for row in range(2):
+            hid_ref[row, :, at] = rounded[row * steps : (row + 1) * steps].astype(BF16)
         hidden[:, at] = rounded
         squares = squares + jnp.sum(rounded * rounded, axis=-1, keepdims=True)
-    final = (hidden[...] * lax.rsqrt(squares / width + EPSILON) * fg_ref[...].astype(F32)).astype(BF16)
+    final = (hidden[...] * lax.rsqrt(squares / width + EPSILON) * fg_ref[...].astype(F32)[None, :]).astype(BF16)
     cands = cand_ref.shape[1]
     logits = jnp.where(
         lax.broadcasted_iota(jnp.int32, (rows8, cands), 0) < steps,
@@ -533,14 +550,19 @@
         dot_nt(final, cand_ref[1]),
     )
     logprob = logits - jnp.log(jnp.sum(jnp.exp(logits), axis=-1, keepdims=True))
-    lpall[me] = jnp.concatenate([logprob, jnp.zeros((rows8, lpall.shape[2] - cands), F32)], axis=1)
+    spaced = jnp.concatenate(
+        [logprob] * steps + [jnp.zeros((rows8, lpall.shape[2] - steps * cands), F32)], axis=1
+    )
+    lane_lp = lax.broadcasted_iota(jnp.int32, spaced.shape, 1)
+    step_lp = lax.rem(lax.broadcasted_iota(jnp.int32, spaced.shape, 0), steps)
+    lpall[me] = jnp.where(lane_lp // cands == step_lp, spaced, 0.0)
     lp_spread[0]()
     lp_spread[1]()
     placed = jnp.dot(
-        pick_ref[...], lpall[...].reshape(rows, lpall.shape[2]),
+        pick[...], lpall[...].reshape(rows, lpall.shape[2]),
         precision=lax.Precision.HIGHEST, preferred_element_type=F32,
     )
-    lp_ref[...] = placed[:, 0:cands]
+    lp_ref[...] = placed[0 : lp_ref.shape[0], 0 : lp_ref.shape[1]]
 
     x_gather[4]()
     b_gather[4]()
@@ -574,14 +596,6 @@
     frequency = ROPE_BASE ** (-np.arange(half, dtype=np.float32) / np.float32(half))
     frequency = jnp.asarray(np.concatenate([frequency, frequency])[None, :].astype(np.float32))
 
-    slot_index = slot_of(row_owner[:, 0], n, CAP)
-    wanted = me * CAP + jnp.arange(CAP, dtype=jnp.int32)
-    select = (slot_index[None, :] == wanted[:, None]).astype(F32)
-    same_step = jnp.eye(step_count, dtype=F32)
-    pick = (select[:, None, :, None] * same_step[None, :, None, :]).reshape(
-        CAP * step_count, row_count * step_count
-    )
-
     chunk = width // CHUNKS
     rows = row_count * step_count
     padded = span + 128
@@ -589,14 +603,14 @@
     smem = pl.BlockSpec(memory_space=pltpu.SMEM)
     hbm = pl.BlockSpec(memory_space=pl.ANY)
     dma = pltpu.SemaphoreType.DMA
-    hidden_out, cand_logprob = pl.pallas_call(
+    return pl.pallas_call(
         fused_kernel,
         out_shape=(
-            jax.ShapeDtypeStruct((rows8, width), BF16),
-            jax.ShapeDtypeStruct((CAP * step_count, cands), F32),
+            jax.ShapeDtypeStruct((row_count // n, step_count, width), BF16),
+            jax.ShapeDtypeStruct((CAP, step_count * cands), F32),
         ),
         in_specs=[vmem, vmem, hbm, hbm, hbm, hbm, vmem, vmem, vmem, vmem, vmem,
-                  vmem, vmem, vmem, vmem, vmem, hbm, hbm, smem, vmem, vmem, vmem, vmem],
+                  hbm, vmem, vmem, hbm, vmem, hbm, hbm, smem, hbm, vmem, vmem, smem],
         out_specs=(vmem, vmem),
         scratch_shapes=[
             pltpu.VMEM((width, qcols), BF16),
@@ -614,6 +628,10 @@
             pltpu.VMEM((rows, 2 * kvcols), F32),
             pltpu.VMEM((rows8, width), F32),
             pltpu.VMEM((rank, width), BF16),
+            pltpu.VMEM(b_query.shape, BF16),
+            pltpu.VMEM((rank, qcols), BF16),
+            pltpu.VMEM(cand_rows.shape, BF16),
+            pltpu.VMEM((8, rows), F32),
             pltpu.VMEM((n, rows8, cols), BF16),
             pltpu.VMEM((n, rows8, cols), BF16),
             pltpu.VMEM((n, rows8, qcols), BF16),
@@ -626,7 +644,7 @@
             pltpu.VMEM((CHUNKS, NZ - 1, rows8, chunk), BF16),
             pltpu.VMEM((rows8, width), F32),
             pltpu.VMEM((n, rows8, 128), F32),
-            dma((8,)),
+            dma((11,)),
             dma((n,)), dma((n,)), dma((n,)), dma((n,)),
             dma((n,)), dma((n,)), dma((n,)), dma((n,)),
             dma((n,)), dma((n,)), dma((n,)), dma((n,)),
@@ -639,14 +657,10 @@
         ),
         name="layer",
     )(
-        x_in.reshape(n, rows8, part), ln_gain[None, :], w_query, w_key.T, w_value.T, w_out,
+        x_in, ln_gain, w_query, w_key.T, w_value.T, w_out,
         q_gain[None, :], k_gain[None, :], a_query.T, a_key.T, a_value.T, b_query, b_key, b_value,
-        a_out.T, b_out, key_cache, value_cache, kv_length, cand_rows, final_gain[None, :],
-        frequency, pick,
-    )
-    return (
-        hidden_out.reshape(row_count // n, step_count, width),
-        cand_logprob.reshape(CAP, step_count * cands),
+        a_out.T, b_out, key_cache, value_cache, kv_length, cand_rows, final_gain,
+        frequency, row_owner[:, 0],
     )
 
 

time: 82.9 us -> 72.9 us (0.88)
  local copies, waits for them, and re-layouts: 7.8 us -> 2.81 us
  Pallas kernels: 71.7 us -> 69.2 us
  other arithmetic: 2.45 us -> 0 us
    reshape x3 -> x0, local copies, waits for them, and re-layouts: 4.47 us -> none  [the longest x1 1.56 us: fused_on_device(): x_in.reshape(n, rows8, part)]
    unnamed x0 -> x2, local copies, waits for them, and re-layouts: none -> 2.81 us
    broadcast_in_dim x2 -> x0, local copies, waits for them, and re-layouts: 2.56 us -> none  [the longest x1 1.32 us: fused_on_device(): final_gain[None, :]]
    pallas_call x1, Pallas kernels: 71.7 us -> 69.2 us  [fused_on_device(): pl.pallas_call(fused_kernel, out_shape=(jax.ShapeDtypeStruct((row_count /...]
    reduce_sum x1 -> x0, other arithmetic: 0.84 us -> none  [slot_of(): return row_owner * capacity + jnp.sum(before * owned_rows, axis=1)]
where the time goes in v2:
time: 72.9 us; the launch traced here: 72.6 us
  Pallas kernels  69.2 us (95%)
  local copies, waits for them, and re-layouts  2.81 us (4%)
    pallas_call x1, Pallas kernels, fused_on_device(): pl.pallas_call(fused_kernel, out_shape=(jax.ShapeDtypeStruct((row_count /...  69.2 us
    unnamed x2, local copies, waits for them, and re-layouts  2.81 us

profile of v2, /device:TPU:0, one launch (start us, length us, event | category | flops | bytes accessed | tf_op | source)
XLA Modules:
  0.0 72.6 jit_solution(7319258142854440641)
XLA Ops:
  0.6 69.2 %layer.1 = (bf16[2,4,5120]{2,1,0:T(4,128)(2,1)}, f32[4,32]{1,0:T(4,128)}) custom-call(bf16[32,4,320]{2,1,0:T(4,128)(2,1)} %x_ref.1, bf16[320]{0:T(512)(128)(2,1)} %gain_ref.1, bf16[5120,512]{1,0:T(8,128)(2,1)} %wq_hbm.1, bf16[64,5120]{1,0:T(8,128)(2,1)} %bitcast.9, bf16[64,5120]{1,0:T(8,128)(2,1)} %bitcast.10, bf16[512,5120]{1,0:T(8,128)(2,1)} %wo_hbm.1, ...), custom_call_target="tpu_custom_call" | custom-call | tf_op jit(solution)/shard_map/layer/pallas_call | solution.py:606
  69.8 1.6 %copy.27 = bf16[2,4,5120]{2,1,0:T(4,128)(2,1)} copy(bf16[2,4,5120]{2,1,0:T(4,128)(2,1)} %get-tuple-element.4) | data formatting | bytes 163840
  71.4 1.3 %copy.28 = f32[4,32]{1,0:T(4,128)} copy(f32[4,32]{1,0:T(4,128)} %get-tuple-element.5) | data formatting | bytes 1024

commit v3 on v2

--- a/solution.py
+++ b/solution.py
@@ -272,9 +272,10 @@
     ball[me] = bo_ref[...]
     pl.semaphore_wait(barrier, n - 1)
 
-    def gather(buffer, send, recv):
+    def gather(buffer, send, recv, low=0, count=None):
         def hop(block, device, number):
-            return remote(buffer.at[block], buffer.at[block], send.at[number], recv.at[block], device)
+            held = buffer.at[block] if count is None else buffer.at[block, pl.ds(low, count)]
+            return remote(held, held, send.at[number], recv.at[block], device)
 
         def begin():
             hop(me, y_peer, 0).start()
@@ -337,7 +338,11 @@
 
         return begin, finish, drain
 
-    x_gather = gather(xall, xs, xr)
+    cut = (groups + 1) // 2
+    x_halves = [
+        gather(xall, xs.at[0], xr.at[0], 0, cut),
+        gather(xall, xs.at[1], xr.at[1], cut, groups + 1 - cut),
+    ]
     b_gather = gather(ball, bs, br)
     low_scatter = exchange(lowp, lowr, l1s, l1r, False)
     low_spread = exchange(lowall, lowall, l2s, l2r, True)
@@ -345,7 +350,8 @@
     att_swap = exchange(atts, attr, ats, atr, False)
     lp_spread = exchange(lpall, lpall, gs, gr, True)
 
-    x_gather[0]()
+    for half in x_halves:
+        half[0]()
 
     own_gained = (own * gain_row).astype(BF16)
     down = jnp.concatenate([aq_ref[...], ak_ref[...], av_ref[...], jnp.zeros((rank, part), BF16)], axis=0)
@@ -383,14 +389,17 @@
         owned = owned + mine
     pick[...] = chosen
 
-    x_gather[1]()
+    for half in x_halves:
+        half[1]()
     low_scatter[1]()
     lowall[me] = jnp.sum(lowr[...], axis=0)
     low_spread[0]()
-    x_gather[2]()
+    for half in x_halves:
+        half[2]()
     for load in loads[:3]:
         load.wait()
-    x_gather[3]()
+    for half in x_halves:
+        half[3]()
     b_gather[0]()
 
     pair = NC * part
@@ -564,7 +573,8 @@
     )
     lp_ref[...] = placed[0 : lp_ref.shape[0], 0 : lp_ref.shape[1]]
 
-    x_gather[4]()
+    for half in x_halves:
+        half[4]()
     b_gather[4]()
     for swap in (low_scatter, low_spread, proj_swap, att_swap, lp_spread):
         swap[2]()
@@ -645,7 +655,7 @@
             pltpu.VMEM((rows8, width), F32),
             pltpu.VMEM((n, rows8, 128), F32),
             dma((11,)),
-            dma((n,)), dma((n,)), dma((n,)), dma((n,)),
+            dma((2, n)), dma((2, n)), dma((n,)), dma((n,)),
             dma((n,)), dma((n,)), dma((n,)), dma((n,)),
             dma((n,)), dma((n,)), dma((n,)), dma((n,)),
             dma((CHUNKS,)), dma((CHUNKS,)), dma((CHUNKS,)), dma((CHUNKS,)),

time: 72.9 us -> 71.7 us (0.984)
  Pallas kernels: 69.2 us -> 68 us
    pallas_call x1, Pallas kernels: 69.2 us -> 68 us  [fused_on_device(): pl.pallas_call(fused_kernel, out_shape=(jax.ShapeDtypeStruct((row_count /...]
where the time goes in v3:
time: 71.7 us; the launch traced here: 71.5 us
  Pallas kernels  68 us (95%)
  local copies, waits for them, and re-layouts  2.81 us (4%)
    pallas_call x1, Pallas kernels, fused_on_device(): pl.pallas_call(fused_kernel, out_shape=(jax.ShapeDtypeStruct((row_count /...  68 us
    unnamed x2, local copies, waits for them, and re-layouts  2.81 us

profile of v3, /device:TPU:0, one launch (start us, length us, event | category | flops | bytes accessed | tf_op | source)
XLA Modules:
  0.0 71.5 jit_solution(2515745193136076439)
XLA Ops:
  0.6 68.0 %layer.1 = (bf16[2,4,5120]{2,1,0:T(4,128)(2,1)}, f32[4,32]{1,0:T(4,128)}) custom-call(bf16[32,4,320]{2,1,0:T(4,128)(2,1)} %x_ref.1, bf16[320]{0:T(512)(128)(2,1)} %gain_ref.1, bf16[5120,512]{1,0:T(8,128)(2,1)} %wq_hbm.1, bf16[64,5120]{1,0:T(8,128)(2,1)} %bitcast.9, bf16[64,5120]{1,0:T(8,128)(2,1)} %bitcast.10, bf16[512,5120]{1,0:T(8,128)(2,1)} %wo_hbm.1, ...), custom_call_target="tpu_custom_call" | custom-call | tf_op jit(solution)/shard_map/layer/pallas_call | solution.py:616
  68.6 1.6 %copy.27 = bf16[2,4,5120]{2,1,0:T(4,128)(2,1)} copy(bf16[2,4,5120]{2,1,0:T(4,128)(2,1)} %get-tuple-element.4) | data formatting | bytes 163840
  70.2 1.3 %copy.28 = f32[4,32]{1,0:T(4,128)} copy(f32[4,32]{1,0:T(4,128)} %get-tuple-element.5) | data formatting | bytes 1024
